TPU v7x, 32 devices: a whole 2x2x4 slice. The times are simulated.
32 devices in a mesh: slab: 2 (over x), xy: 8 (over z, y), gz: 2 (over core).
Axes of the slice: x: 2, y: 2, z: 4, core: 2. Of those that a mesh axis runs over, the one named last changes fastest.
Arguments:
- source_rows: bfloat16 [32768, 128], P(('slab', 'xy', 'gz')), parts along dimension 0, may hold values from 0 to 1
- interp_bank: bfloat16 [2, 16, 128, 256], replicated, may hold values from -0.375 to 0.375
- source_taps: int32 [2, 65536], P(None, ('slab', 'xy', 'gz')), parts along dimension 1, may hold values from 0 to 1023
- tap_phase: int32 [2, 65536], P(None, ('slab', 'xy', 'gz')), parts along dimension 1, may hold values from 0 to 15
- mesh_node: int32 [65536], P(('slab', 'xy', 'gz')), parts along dimension 0, may hold values from 0 to 127
- target_tile: int32 [65536, 1], P(('slab', 'xy', 'gz')), parts along dimension 0, may hold values from 0 to 15; in each aligned block of 2048 rows (0 to 2047, 2048 to 4095, ...) at most 256 rows name the same one
- target_row: int32 [65536], P(('slab', 'xy', 'gz')), parts along dimension 0, may hold values from 0 to 1023
- tile_owner: int32 [32], P('slab'), parts along dimension 0, may hold values from 0 to 15, each once
- coarse_mesh: float32 [4, 2, 128], P(('slab', 'gz'), None, 'xy'), parts along dimension 0, may hold values from 0 to 1
Outputs:
- blended: bfloat16 [32768, 128], P(('slab', 'xy', 'gz')), parts along dimension 0
There are 2 independent parts, one for each index of `slab`. A program takes and returns all parts, laid end to end along the dimension named above; an argument that names none is the same for every part. Nothing has to cross between parts.
Inputs may be any that keep to these rules, and one draw needn't show every extreme that they name: `target_tile`: among the 2048 contributions of one device, at most 256 intersect any one output tile, and some tile is intersected by exactly 256 of them. `tile_owner`: each device index owns exactly one output tile.
All inputs are finite; a program needn't handle non-finite values.
Results may differ from a plain program's by a relative error of at most 0.0057.
Values may be sent and summed in bfloat16 or wider, within the bound.
A program may use at most 64 MiB of HBM per device.

v0:
```python
import jax
import jax.numpy as jnp
from jax import lax
from jax.sharding import PartitionSpec as P

floor_weight = 0.1


def on_device(
    source_rows,
    interp_bank,
    source_taps,
    tap_phase,
    mesh_node,
    target_tile,
    target_row,
    tile_owner,
    coarse_mesh,
):
    contrib = mesh_node.shape[0]
    voxels = source_rows.shape[1]
    tap_count = interp_bank.shape[0]
    phases = interp_bank.shape[1]
    plane_size = lax.axis_size("xy")
    group_size = lax.axis_size("gz")
    owners = plane_size * group_size
    capacity = 2 * contrib // owners
    tile_rows = contrib // 2
    spread = float(voxels // 4)
    gathered = lax.all_gather(coarse_mesh, "xy", axis=2, tiled=True)
    columns = gathered.shape[2]
    selector = (mesh_node[None, :] == lax.iota(jnp.int32, columns)[:, None]).astype(jnp.float32)
    looked = jnp.dot(
        gathered[0], selector, precision=lax.Precision.HIGHEST, preferred_element_type=jnp.float32
    )
    block_rows = min(512, contrib)
    blocks = contrib // block_rows
    tap_blocks = source_taps.reshape(tap_count, blocks, block_rows).transpose(1, 0, 2)
    phase_blocks = tap_phase.reshape(tap_count, blocks, block_rows).transpose(1, 0, 2)
    shift_blocks = looked[0].reshape(blocks, block_rows)
    stacked = interp_bank.reshape(tap_count * phases * voxels, 2 * voxels)
    phase_ids = lax.iota(jnp.int32, phases)

    def resample(inputs):
        taps_here, phase_here, shift_here = inputs
        placed = []
        for tap_index in range(tap_count):
            picked = jnp.take(source_rows, taps_here[tap_index], axis=0)
            selector = (phase_here[tap_index][:, None] == phase_ids[None, :]).astype(jnp.bfloat16)
            placed.append(
                (picked[:, None, :] * selector[:, :, None]).reshape(block_rows, phases * voxels)
            )
        widened = jnp.concatenate(placed, axis=1)
        products = jnp.dot(widened, stacked, preferred_element_type=jnp.float32)
        weight = shift_here[:, None]
        return ((1.0 - weight) * products[:, :voxels] + weight * products[:, voxels:]).astype(
            jnp.bfloat16
        )

    mixed = lax.map(resample, (tap_blocks, phase_blocks, shift_blocks)).reshape(contrib, voxels)
    centers = ((voxels - 1) * looked[1]).astype(jnp.bfloat16)
    owner_ids = lax.iota(jnp.int32, owners)
    tiles = target_tile[:, 0]
    owner_of = jnp.sum(
        jnp.where(tiles[:, None] == owner_ids[None, :], tile_owner[None, :], 0), axis=1
    )
    member = (owner_of[:, None] == owner_ids[None, :]).astype(jnp.int32)
    earlier = jnp.cumsum(member, axis=0) - member
    position = jnp.sum(earlier * member, axis=1)
    slot_of = owner_of * capacity + position
    values = jnp.zeros((owners * capacity, voxels), jnp.bfloat16).at[slot_of].set(mixed)
    sent_centers = jnp.zeros((owners * capacity,), jnp.bfloat16).at[slot_of].set(centers)
    sent_rows = jnp.full((owners * capacity,), tile_rows, jnp.int32).at[slot_of].set(target_row)
    got_values, got_centers, got_rows = (
        lax.all_to_all(
            values.reshape(owners, capacity, voxels),
            ("xy", "gz"),
            split_axis=0,
            concat_axis=0,
            tiled=True,
        ),
        lax.all_to_all(
            sent_centers.reshape(owners, capacity),
            ("xy", "gz"),
            split_axis=0,
            concat_axis=0,
            tiled=True,
        ),
        lax.all_to_all(
            sent_rows.reshape(owners, capacity),
            ("xy", "gz"),
            split_axis=0,
            concat_axis=0,
            tiled=True,
        ),
    )
    flat_values = got_values.reshape(owners * capacity, voxels).astype(jnp.float32)
    flat_centers = got_centers.reshape(owners * capacity).astype(jnp.float32)
    flat_rows = got_rows.reshape(owners * capacity)
    offsets = lax.iota(jnp.float32, voxels)[None, :] - flat_centers[:, None]
    weights = jnp.exp(-0.5 * (offsets / spread) ** 2)
    operand = jnp.concatenate([weights * flat_values, weights], axis=1)
    one_hot = (lax.iota(jnp.int32, tile_rows)[:, None] == flat_rows[None, :]).astype(jnp.float32)
    sums = jnp.dot(
        one_hot, operand, precision=lax.Precision.HIGHEST, preferred_element_type=jnp.float32
    )
    result = sums[:, :voxels] / jnp.maximum(sums[:, voxels:], floor_weight)
    return result.astype(jnp.bfloat16)


def solution(mesh):
    return jax.shard_map(
        on_device,
        mesh=mesh,
        in_specs=(
            P(("slab", "xy", "gz"), None),
            P(),
            P(None, ("slab", "xy", "gz")),
            P(None, ("slab", "xy", "gz")),
            P(("slab", "xy", "gz")),
            P(("slab", "xy", "gz"), None),
            P(("slab", "xy", "gz")),
            P("slab"),
            P(("slab", "gz"), None, "xy"),
        ),
        out_specs=P(("slab", "xy", "gz"), None),
        check_vma=False,
    )
```

profile of v0, /device:TPU:0, one launch (start us, length us, event | category | flops | bytes accessed | tf_op | source)
XLA Modules:
  0.0 179.4 jit_solution(285762192476116084)
XLA Ops:
  0.8 4.5 %reduce-window.6 = s32[16,16,128]{2,1,0:T(8,128)S(1)} reduce-window(s32[16,16,128]{2,1,0:T(8,128)S(1)} %fusion.26, s32[]{:T(128)} %constant.11.clone.1), window={size=1x1x128 pad=0_0x0_0x127_0}, to_apply=%region_1.2 | reduce-window | flops 4161536 | bytes 262148 | tf_op jit(solution)/shard_map/reduce-window
  7.0 32.3 %all_gather.3 = f32[1,2,128]{1,0,2:T(1,128)S(1)} all-gather(f32[1,2,16]{1,0,2:T(1,128)S(1)} %copy.14), channel_id=1, replica_groups=mesh['slab'=2,'xy'=8,'gz'=2] {'xy'}, dimensions={2}, use_global_device_ids=true | all-gather | bytes 1152 | tf_op jit(solution)/shard_map/all_gather | solution.py:30
  40.4 14.6 %scatter_custom_fusion.1 = bf16[4096]{0:T(1024)(128)(2,1)S(1)} fusion(s32[2048]{0:T(1024)S(1)} %bitcast.103, bf16[2048]{0:T(1024)(128)(2,1)S(1)} %fusion.30, bf16[]{:T(256)} %constant.14.clone.1), kind=kCustom, calls=%fused_computation.74 | custom fusion | bytes 8194 | tf_op jit(solution)/shard_map/scatter | solution.py:72
  56.8 5.6 %all-to-all-start.1 = ((bf16[16,2,128]{2,1,0:T(2,128)(2,1)}), bf16[16,2,128]{2,1,0:T(2,128)(2,1)S(1)}, u32[]{:S(2)}, u32[]{:S(2)}) async-start(bf16[16,2,128]{2,1,0:T(2,128)(2,1)} %reshape.245), calls=%async_computation.1 | async-start | bytes 16384 | tf_op jit(solution)/shard_map/all_to_all | solution.py:82
  62.5 57.4 %while.12 = (s32[]{:T(128)}, bf16[4,512,128]{2,1,0:T(8,128)(2,1)S(1)}, f32[4,512]{1,0:T(4,128)S(1)}, s32[4,2,512]{2,1,0:T(2,128)}, bf16[1024,128]{1,0:T(8,128)(2...) while((s32[]{:T(128)}, ...), condition=%wide.region_7.9_spmd.clone.clone, body=%wide.region_6.8_spmd.clone.clone.sunk | while | flops 1084665344 | bytes 30996664 | solution.py:60
  63.3 2.0 %gather_fusion.1 = bf16[512,128]{1,0:T(8,128)(2,1)S(1)} fusion(bf16[1024,128]{1,0:T(8,128)(2,1)} %get-tuple-element.185, s32[1024]{0:T(1024)S(1)} %pad_clamp_fusion.5), kind=kCustom, calls=%fused_computation.clone.clone.1 | custom fusion | bytes 264192 | tf_op jit(solution)/shard_map/while/body/eval_jaxpr/jit(_take)/gather | solution.py:48
  65.7 2.7 %broadcast_multiply_fusion.5 = bf16[512,16,128]{2,1,0:T(8,128)(2,1)S(1)} fusion(bf16[512,16]{1,0:T(8,128)(2,1)S(1)} %copy.30, bf16[512,128]{1,0:T(8,128)(2,1)S(1)} %broadcast_select_fusion.5), kind=kLoop, calls=%fused_computation.13.clone.1 | loop fusion | flops 1048576 | bytes 2244608 | tf_op jit(solution)/shard_map/while/body/eval_jaxpr/mul | solution.py:51
  69.3 1.3 gather_fusion
  71.0 2.7 %broadcast_multiply_fusion.4 = bf16[512,16,128]{2,1,0:T(8,128)(2,1)S(1)} fusion(bf16[512,16]{1,0:T(8,128)(2,1)S(1)} %copy.28, bf16[512,128]{1,0:T(8,128)(2,1)S(1)} %broadcast_select_fusion.4), kind=kLoop, calls=%fused_computation.12.clone.1 | loop fusion | flops 1048576 | bytes 2244608 | tf_op jit(solution)/shard_map/while/body/eval_jaxpr/mul | solution.py:51
  75.2 1.3 fusion.46
  77.7 2.0 %gather_fusion.1 = bf16[512,128]{1,0:T(8,128)(2,1)S(1)} fusion(bf16[1024,128]{1,0:T(8,128)(2,1)} %get-tuple-element.185, s32[1024]{0:T(1024)S(1)} %pad_clamp_fusion.5), kind=kCustom, calls=%fused_computation.clone.clone.1 | custom fusion | bytes 264192 | tf_op jit(solution)/shard_map/while/body/eval_jaxpr/jit(_take)/gather | solution.py:48
  80.0 2.7 %broadcast_multiply_fusion.5 = bf16[512,16,128]{2,1,0:T(8,128)(2,1)S(1)} fusion(bf16[512,16]{1,0:T(8,128)(2,1)S(1)} %copy.30, bf16[512,128]{1,0:T(8,128)(2,1)S(1)} %broadcast_select_fusion.5), kind=kLoop, calls=%fused_computation.13.clone.1 | loop fusion | flops 1048576 | bytes 2244608 | tf_op jit(solution)/shard_map/while/body/eval_jaxpr/mul | solution.py:51
  83.7 1.3 gather_fusion
  85.3 2.7 %broadcast_multiply_fusion.4 = bf16[512,16,128]{2,1,0:T(8,128)(2,1)S(1)} fusion(bf16[512,16]{1,0:T(8,128)(2,1)S(1)} %copy.28, bf16[512,128]{1,0:T(8,128)(2,1)S(1)} %broadcast_select_fusion.4), kind=kLoop, calls=%fused_computation.12.clone.1 | loop fusion | flops 1048576 | bytes 2244608 | tf_op jit(solution)/shard_map/while/body/eval_jaxpr/mul | solution.py:51
  89.6 1.3 fusion.46
  92.0 2.0 %gather_fusion.1 = bf16[512,128]{1,0:T(8,128)(2,1)S(1)} fusion(bf16[1024,128]{1,0:T(8,128)(2,1)} %get-tuple-element.185, s32[1024]{0:T(1024)S(1)} %pad_clamp_fusion.5), kind=kCustom, calls=%fused_computation.clone.clone.1 | custom fusion | bytes 264192 | tf_op jit(solution)/shard_map/while/body/eval_jaxpr/jit(_take)/gather | solution.py:48
  94.4 2.7 %broadcast_multiply_fusion.5 = bf16[512,16,128]{2,1,0:T(8,128)(2,1)S(1)} fusion(bf16[512,16]{1,0:T(8,128)(2,1)S(1)} %copy.30, bf16[512,128]{1,0:T(8,128)(2,1)S(1)} %broadcast_select_fusion.5), kind=kLoop, calls=%fused_computation.13.clone.1 | loop fusion | flops 1048576 | bytes 2244608 | tf_op jit(solution)/shard_map/while/body/eval_jaxpr/mul | solution.py:51
  98.0 1.3 gather_fusion
  99.6 2.7 %broadcast_multiply_fusion.4 = bf16[512,16,128]{2,1,0:T(8,128)(2,1)S(1)} fusion(bf16[512,16]{1,0:T(8,128)(2,1)S(1)} %copy.28, bf16[512,128]{1,0:T(8,128)(2,1)S(1)} %broadcast_select_fusion.4), kind=kLoop, calls=%fused_computation.12.clone.1 | loop fusion | flops 1048576 | bytes 2244608 | tf_op jit(solution)/shard_map/while/body/eval_jaxpr/mul | solution.py:51
  103.9 1.3 fusion.46
  106.3 2.0 %gather_fusion.1 = bf16[512,128]{1,0:T(8,128)(2,1)S(1)} fusion(bf16[1024,128]{1,0:T(8,128)(2,1)} %get-tuple-element.185, s32[1024]{0:T(1024)S(1)} %pad_clamp_fusion.5), kind=kCustom, calls=%fused_computation.clone.clone.1 | custom fusion | bytes 264192 | tf_op jit(solution)/shard_map/while/body/eval_jaxpr/jit(_take)/gather | solution.py:48
  108.7 2.7 %broadcast_multiply_fusion.5 = bf16[512,16,128]{2,1,0:T(8,128)(2,1)S(1)} fusion(bf16[512,16]{1,0:T(8,128)(2,1)S(1)} %copy.30, bf16[512,128]{1,0:T(8,128)(2,1)S(1)} %broadcast_select_fusion.5), kind=kLoop, calls=%fused_computation.13.clone.1 | loop fusion | flops 1048576 | bytes 2244608 | tf_op jit(solution)/shard_map/while/body/eval_jaxpr/mul | solution.py:51
  112.3 1.3 gather_fusion
  114.0 2.7 %broadcast_multiply_fusion.4 = bf16[512,16,128]{2,1,0:T(8,128)(2,1)S(1)} fusion(bf16[512,16]{1,0:T(8,128)(2,1)S(1)} %copy.28, bf16[512,128]{1,0:T(8,128)(2,1)S(1)} %broadcast_select_fusion.4), kind=kLoop, calls=%fused_computation.12.clone.1 | loop fusion | flops 1048576 | bytes 2244608 | tf_op jit(solution)/shard_map/while/body/eval_jaxpr/mul | solution.py:51
  119.9 6.8 %scatter_custom_fusion.2 = bf16[4096,128]{1,0:T(8,128)(2,1)} fusion(s32[2048]{0:T(1024)S(1)} %bitcast.104, bf16[2048,128]{1,0:T(8,128)(2,1)S(1)} %bitcast.107, bf16[]{:T(256)} %constant.14.clone.1), kind=kCustom, calls=%fused_computation.52 | custom fusion | bytes 1048578 | tf_op jit(solution)/shard_map/scatter | solution.py:71
  126.7 6.0 %all-to-all-start.2 = ((bf16[16,256,128]{2,1,0:T(8,128)(2,1)}), bf16[16,256,128]{2,1,0:T(8,128)(2,1)S(1)}, u32[]{:S(2)}, u32[]{:S(2)}) async-start(bf16[16,256,128]{2,1,0:T(8,128)(2,1)} %bitcast.16), calls=%async_computation.2 | async-start | bytes 2097152 | tf_op jit(solution)/shard_map/all_to_all | solution.py:75
  132.7 8.8 %scatter_custom_fusion = s32[4096]{0:T(1024)} fusion(s32[2048]{0:T(1024)S(1)} %bitcast.105, s32[2048]{0:T(1024)} %param.19, s32[]{:T(128)} %constant.10.clone.1), kind=kCustom, calls=%fused_computation.71 | custom fusion | bytes 16896 | tf_op jit(solution)/shard_map/scatter | solution.py:73
  141.5 14.1 %all-to-all-done.2 = bf16[16,256,128]{2,1,0:T(8,128)(2,1)S(1)} async-done(((bf16[16,256,128]{2,1,0:T(8,128)(2,1)}), bf16[16,256,128]{2,1,0:T(8,128)(2,1)S(1)}, u32[]{:S(2)}, u32[]{:S(2)}) %all-to-all-start.2) | async-done | bytes 1048608 | tf_op jit(solution)/shard_map/all_to_all | solution.py:75
  155.6 6.9 %all-to-all-start = ((s32[16,1,256]{2,1,0:T(1,128)}), s32[16,1,256]{2,1,0:T(1,128)S(1)}, u32[]{:S(2)}, u32[]{:S(2)}) async-start(s32[16,1,256]{2,1,0:T(1,128)} %bitcast.5), calls=%async_computation | async-start | bytes 32768 | tf_op jit(solution)/shard_map/all_to_all | solution.py:89
  162.5 1.8 %convert_multiply_fusion = (f32[4096,128]{1,0:T(8,128)S(1)}, f32[4096,128]{1,0:T(8,128)}) fusion(bf16[16,256,128]{2,1,0:T(8,128)(2,1)S(1)} %all-to-all-done.2, f32[4096]{0:T(1024)S(1)} %bitcast.95), kind=kLoop, calls=%fused_computation.46 | loop fusion | flops 3145728 | bytes 5259264 | tf_op jit(solution)/shard_map/mul | solution.py:102
  164.4 4.6 %all-to-all-done = s32[16,1,256]{2,1,0:T(1,128)S(1)} async-done(((s32[16,1,256]{2,1,0:T(1,128)}), s32[16,1,256]{2,1,0:T(1,128)S(1)}, u32[]{:S(2)}, u32[]{:S(2)}) %all-to-all-start) | async-done | bytes 16416 | tf_op jit(solution)/shard_map/all_to_all | solution.py:89
  169.0 9.6 %fusion.13 = f32[1024,256]{1,0:T(8,128)S(1)} fusion(s32[4096]{0:T(1024)S(1)} %bitcast.101, f32[4096,128]{1,0:T(8,128)} %get-tuple-element.109, f32[4096,128]{1,0:T(8,128)S(1)} %get-tuple-element.108), kind=kOutput, calls=%fused_computation.40 | convolution fusion | flops 12890144768 | bytes 5259264 | tf_op jit(solution)/shard_map/dot_general | solution.py:104
  (111 shorter events, 24.0 us)
Async XLA Ops:
  56.8 69.9 %all-to-all-start.1 = ((bf16[16,2,128]{2,1,0:T(2,128)(2,1)}), bf16[16,2,128]{2,1,0:T(2,128)(2,1)S(1)}, u32[]{:S(2)}, u32[]{:S(2)}) async-start(bf16[16,2,128]{2,1,0:T(2,128)(2,1)} %reshape.245), calls=%async_computation.1 | async-start | bytes 16384 | tf_op jit(solution)/shard_map/all_to_all | solution.py:82
  68.4 1.0 copy-start
  73.7 1.6 copy-start.1
  82.7 1.0 copy-start
  88.0 1.6 copy-start.1
  97.1 1.0 copy-start
  102.3 1.6 copy-start.1
  111.4 1.0 copy-start
  116.7 1.6 copy-start.1
  126.7 28.9 %all-to-all-start.2 = ((bf16[16,256,128]{2,1,0:T(8,128)(2,1)}), bf16[16,256,128]{2,1,0:T(8,128)(2,1)S(1)}, u32[]{:S(2)}, u32[]{:S(2)}) async-start(bf16[16,256,128]{2,1,0:T(8,128)(2,1)} %bitcast.16), calls=%async_computation.2 | async-start | bytes 2097152 | tf_op jit(solution)/shard_map/all_to_all | solution.py:75
  155.6 13.4 %all-to-all-start = ((s32[16,1,256]{2,1,0:T(1,128)}), s32[16,1,256]{2,1,0:T(1,128)S(1)}, u32[]{:S(2)}, u32[]{:S(2)}) async-start(s32[16,1,256]{2,1,0:T(1,128)} %bitcast.5), calls=%async_computation | async-start | bytes 32768 | tf_op jit(solution)/shard_map/all_to_all | solution.py:89
where the time goes:
time: 180 us; the launch traced here: 179 us
  local copies, waits for them, and re-layouts  60.2 us (33%)
  other arithmetic  33 us (18%)
  blocking collectives  32.3 us (18%)
  waiting for transfers between devices  18.8 us (10%)
  starting transfers between devices  18.5 us (10%)
  matrix products  15.8 us (9%)
    all_gather x1, blocking collectives, on_device(): gathered = lax.all_gather(coarse_mesh, 'xy', axis=2, tiled=True)  32.3 us
    mul x8, other arithmetic, resample(): picked[:, None, :] * selector[:, :, None]  21.5 us
    scatter x1, local copies, waits for them, and re-layouts, on_device(): jnp.zeros((owners * capacity,), jnp.bfloat16).at[slot_of].set(centers)  14.6 us
    all_to_all x1, waiting for transfers between devices, on_device(): lax.all_to_all(values.reshape(owners, capacity, voxels), ('xy', 'gz'), sp...  14.1 us
    gather x8, local copies, waits for them, and re-layouts, resample(): picked = jnp.take(source_rows, taps_here[tap_index], axis=0)  13.5 us
    while x24, local copies, waits for them, and re-layouts  9.97 us
    dot_general x1, matrix products, on_device(): jnp.dot(one_hot, operand, precision=lax.Precision.HIGHEST, preferred_elem...  9.59 us
    scatter x1, local copies, waits for them, and re-layouts, on_device(): jnp.full((owners * capacity,), tile_rows, jnp.int32).at[slot_of]  8.79 us
  transfers between devices with their start and end apart: 3, of which 2 were waited for; matrix products, arithmetic and copies ran while one was open for 38% of the time, Pallas kernels for 0%

commit v1 on v0

v1 whole, which is shorter than its diff:
```python
import functools

import jax
import jax.numpy as jnp
from jax import lax
from jax.experimental import pallas as pl
from jax.experimental.pallas import tpu as pltpu
from jax.sharding import PartitionSpec as P

floor_weight = 0.1
LANES = 128
INFO = 16
MESH_ROW = 6
META = 16
f32, bf16, i32 = jnp.float32, jnp.bfloat16, jnp.int32
NT = (((1,), (1,)), ((), ()))


def flip(a, b, count):
    out, bit = 0, 1
    while bit < count:
        out = out + ((a // bit + b // bit) % 2) * bit
        bit *= 2
    return out


def one_hot(columns, values):
    return jnp.where(columns == values, 1.0, 0.0).astype(bf16)


def kernel(
    sizes,
    source_ref, bank_hbm, taps_ref, phase_ref, node_ref, tile_ref, row_ref, owner_ref, mesh_ref,
    out_ref,
    bank, member, info_rows, info_all, placed, acc, mesh_own, mesh_got, sent, got,
    bank_sem, mesh_send, mesh_recv, send_sem, recv_sem,
):
    contrib, owners, plane, group, cap, wide, nodes = sizes
    voxels = source_ref.shape[1]
    rows_src = source_ref.shape[0]
    tile_rows = out_ref.shape[0]
    phases = placed.shape[1] // (2 * voxels)
    spread = float(voxels // 4)
    slab_at, xy_at, gz_at = lax.axis_index("slab"), lax.axis_index("xy"), lax.axis_index("gz")
    me = xy_at * group + gz_at

    def device(step):
        other = flip(me, step, owners)
        return (slab_at, other // group, other % group)

    barrier = pltpu.get_barrier_semaphore()

    @pl.loop(1, owners)
    def _(step):
        pl.semaphore_signal(barrier, inc=1, device_id=device(step), device_id_type=pl.DeviceIdType.MESH)

    bank_copy = pltpu.make_async_copy(bank_hbm, bank, bank_sem)
    bank_copy.start()

    part = mesh_ref.shape[2]
    place = jnp.where(
        lax.broadcasted_iota(i32, (part, nodes), 1) == lax.broadcasted_iota(i32, (part, nodes), 0) + xy_at * part, 1.0, 0.0
    )
    mesh_own[...] = jnp.dot(mesh_ref[0], place, precision=lax.Precision.HIGHEST, preferred_element_type=f32)

    pl.semaphore_wait(barrier, owners - 1)

    def mesh_copy(step):
        return pltpu.make_async_remote_copy(
            src_ref=mesh_own,
            dst_ref=mesh_got.at[step],
            send_sem=mesh_send.at[step],
            recv_sem=mesh_recv.at[step],
            device_id=(slab_at, flip(xy_at, step, plane), gz_at),
            device_id_type=pl.DeviceIdType.MESH,
        )

    @pl.loop(1, plane)
    def _(step):
        mesh_copy(step).start()

    tiles = tile_ref[...]
    owner = jnp.zeros_like(tiles)
    for tile in range(owners):
        owner = jnp.where(tiles == tile, owner_ref[tile], owner)
    relative = jnp.bitwise_xor(owner, me)
    chosen = jnp.where(lax.broadcasted_iota(i32, (owners, contrib), 0) == relative, 1.0, 0.0)
    member[...] = chosen
    chunk = 256
    before = (
        lax.broadcasted_iota(i32, (chunk, chunk), 0) < lax.broadcasted_iota(i32, (chunk, chunk), 1)
    ).astype(f32).astype(bf16)
    carry = jnp.zeros((owners, 1), f32)
    ranks = []
    for at in range(0, contrib, chunk):
        here = chosen[:, at : at + chunk]
        earlier = jnp.dot(here.astype(bf16), before, preferred_element_type=f32) + carry
        ranks.append(jnp.sum(here * earlier, axis=0, keepdims=True))
        carry = carry + jnp.sum(here, axis=1, keepdims=True)
    rank = jnp.concatenate(ranks, axis=1)
    rank_hot = one_hot(lax.broadcasted_iota(i32, (wide, contrib), 0).astype(f32), rank)
    node_hot = one_hot(lax.broadcasted_iota(i32, (nodes, contrib), 0), node_ref[...])

    @pl.loop(1, plane)
    def _(step):
        mesh_copy(step).wait_recv()

    mesh = mesh_own[...]
    for step in range(1, plane):
        mesh = mesh + mesh_got[step]
    shift, center = mesh[0:1], (voxels - 1) * mesh[1:2]
    high = shift.astype(bf16).astype(f32)
    middle = (shift - high).astype(bf16).astype(f32)
    low = shift - high - middle
    spot = lax.broadcasted_iota(i32, (INFO, nodes), 0)
    table = jnp.zeros((INFO, nodes), f32)
    for at, line in enumerate((high, middle, low, center)):
        table = jnp.where(spot == MESH_ROW + at, line, table)
    info = jnp.dot(table.astype(bf16), node_hot, preferred_element_type=f32)
    target = row_ref[...] + 1
    taps0, taps1 = taps_ref[0:1, :], taps_ref[1:2, :]
    lines = {
        0: taps0 // 256, 1: taps0 % 256, 2: taps1 // 256, 3: taps1 % 256,
        4: phase_ref[0:1, :], 5: phase_ref[1:2, :],
        10: target // 256, 11: target % 256,
    }
    spot = lax.broadcasted_iota(i32, (INFO, contrib), 0)
    for at, line in lines.items():
        info = jnp.where(spot == at, line.astype(f32), info)

    @pl.loop(0, owners)
    def _(step):
        info_rows[pl.ds(pl.multiple_of(step * INFO, INFO), INFO), :] = (
            info * member[pl.ds(step, 1), :]
        ).astype(bf16)

    info_all[...] = lax.dot_general(info_rows[...], rank_hot, NT, preferred_element_type=f32)
    acc[...] = jnp.zeros_like(acc)
    bank_copy.wait()

    def value_copy(step):
        return pltpu.make_async_remote_copy(
            src_ref=sent.at[step],
            dst_ref=got.at[step],
            send_sem=send_sem.at[step],
            recv_sem=recv_sem.at[step],
            device_id=device(step),
            device_id_type=pl.DeviceIdType.MESH,
        )

    bundle = max(1, 256 // cap)
    size = bundle * cap
    lines_each = wide // LANES

    def produce(first):
        pieces = []
        for d in range(bundle):
            lanes = info_all[pl.ds(pl.multiple_of((first + d) * INFO, INFO), INFO), :]
            pieces.append(lanes.T[:cap])
            meta = [lanes[r : r + 1, at * LANES : (at + 1) * LANES] for r in (9, 10, 11) for at in range(lines_each)]
            spot = lax.broadcasted_iota(i32, (META, LANES), 0)
            filled = jnp.zeros((META, LANES), f32)
            for at, line in enumerate(meta):
                filled = jnp.where(spot == at, line, filled)
            sent[first + d, cap : cap + META, :] = filled.astype(bf16)
        columns = pieces[0] if bundle == 1 else jnp.concatenate(pieces, axis=0)
        source = source_ref[...]
        ids = lax.broadcasted_iota(i32, (size, rows_src), 1).astype(f32)
        for k in range(2):
            tap = columns[:, 2 * k : 2 * k + 1] * 256.0 + columns[:, 2 * k + 1 : 2 * k + 2]
            picked = jnp.dot(one_hot(ids, tap), source, preferred_element_type=f32).astype(bf16)
            phase = jnp.broadcast_to(columns[:, 4 + k : 5 + k], (size, voxels)).astype(bf16)
            for p in range(phases):
                at = (k * phases + p) * voxels
                placed[:, at : at + voxels] = jnp.where(phase == jnp.bfloat16(p), picked, jnp.bfloat16(0))
        products = jnp.dot(placed[...], bank[...], preferred_element_type=f32)
        weight = columns[:, MESH_ROW : MESH_ROW + 1] + columns[:, MESH_ROW + 1 : MESH_ROW + 2]
        weight = weight + columns[:, MESH_ROW + 2 : MESH_ROW + 3]
        mixed = ((1.0 - weight) * products[:, :voxels] + weight * products[:, voxels:]).astype(bf16)
        for d in range(bundle):
            sent[first + d, :cap, :] = mixed[d * cap : (d + 1) * cap]

            @pl.when(first + d > 0)
            def _():
                value_copy(first + d).start()

    def consume(values, meta):
        meta = meta.astype(f32)
        target = meta[lines_each : 2 * lines_each] * 256.0 + meta[2 * lines_each : 3 * lines_each]
        target = jnp.concatenate([target[at : at + 1] for at in range(lines_each)], axis=1)[:, :cap]
        turned = meta.T
        center = jnp.concatenate([turned[:, at : at + 1] for at in range(lines_each)], axis=0)[:cap]
        offsets = lax.broadcasted_iota(i32, (cap, voxels), 1).astype(f32) - center
        weights = jnp.exp(-0.5 * (offsets / spread) ** 2)
        operand = jnp.concatenate([weights * values.astype(f32), weights], axis=1).astype(bf16)
        ids = lax.broadcasted_iota(i32, (tile_rows, cap), 0).astype(f32) + 1.0
        acc[...] += jnp.dot(one_hot(ids, target), operand, preferred_element_type=f32)

    blocks = owners // bundle

    @pl.loop(0, blocks)
    def _(turn):
        produce((blocks - 1 - turn) * bundle)

    consume(sent[0, :cap, :], sent[0, cap : cap + META, :])

    @pl.loop(1, owners)
    def _(turn):
        step = owners - turn
        value_copy(step).wait_recv()
        consume(got[step, :cap, :], got[step, cap : cap + META, :])

    out_ref[...] = (acc[:, :voxels] / jnp.maximum(acc[:, voxels:], floor_weight)).astype(bf16)

    @pl.loop(1, plane)
    def _(step):
        mesh_copy(step).wait_send()

    @pl.loop(1, owners)
    def _(step):
        value_copy(step).wait_send()


def on_device(
    source_rows,
    interp_bank,
    source_taps,
    tap_phase,
    mesh_node,
    target_tile,
    target_row,
    tile_owner,
    coarse_mesh,
):
    contrib = mesh_node.shape[0]
    voxels = source_rows.shape[1]
    taps, phases = interp_bank.shape[:2]
    plane = lax.axis_size("xy")
    group = lax.axis_size("gz")
    owners = plane * group
    cap = 2 * contrib // owners
    wide = max(cap, LANES)
    tile_rows = contrib // 2
    nodes = plane * coarse_mesh.shape[2]
    bundle = max(1, 256 // cap)
    vmem = pl.BlockSpec(memory_space=pltpu.VMEM)
    return pl.pallas_call(
        functools.partial(kernel, (contrib, owners, plane, group, cap, wide, nodes)),
        out_shape=jax.ShapeDtypeStruct((tile_rows, voxels), bf16),
        in_specs=[vmem, pl.BlockSpec(memory_space=pl.ANY)] + [vmem] * 5
        + [pl.BlockSpec(memory_space=pltpu.SMEM), vmem],
        out_specs=vmem,
        scratch_shapes=[
            pltpu.VMEM((taps * phases * voxels, 2 * voxels), bf16),
            pltpu.VMEM((owners, contrib), f32),
            pltpu.VMEM((owners * INFO, contrib), bf16),
            pltpu.VMEM((owners * INFO, wide), f32),
            pltpu.VMEM((bundle * cap, taps * phases * voxels), bf16),
            pltpu.VMEM((tile_rows, 2 * voxels), f32),
            pltpu.VMEM((2, nodes), f32),
            pltpu.VMEM((plane, 2, nodes), f32),
            pltpu.VMEM((owners, cap + META, voxels), bf16),
            pltpu.VMEM((owners, cap + META, voxels), bf16),
            pltpu.SemaphoreType.DMA,
            pltpu.SemaphoreType.DMA((plane,)),
            pltpu.SemaphoreType.DMA((plane,)),
            pltpu.SemaphoreType.DMA((owners,)),
            pltpu.SemaphoreType.DMA((owners,)),
        ],
        compiler_params=pltpu.CompilerParams(
            collective_id=0, has_side_effects=True, vmem_limit_bytes=56 * 1024 * 1024
        ),
    )(
        source_rows,
        interp_bank.reshape(taps * phases * voxels, 2 * voxels),
        source_taps,
        tap_phase,
        mesh_node.reshape(1, contrib),
        target_tile.reshape(1, contrib),
        target_row.reshape(1, contrib),
        tile_owner,
        coarse_mesh,
    )


def solution(mesh):
    return jax.shard_map(
        on_device,
        mesh=mesh,
        in_specs=(
            P(("slab", "xy", "gz"), None),
            P(),
            P(None, ("slab", "xy", "gz")),
            P(None, ("slab", "xy", "gz")),
            P(("slab", "xy", "gz")),
            P(("slab", "xy", "gz"), None),
            P(("slab", "xy", "gz")),
            P("slab"),
            P(("slab", "gz"), None, "xy"),
        ),
        out_specs=P(("slab", "xy", "gz"), None),
        check_vma=False,
    )
```

time: 180 us -> 49.4 us (0.27)
  local copies, waits for them, and re-layouts: 60.2 us -> 1.67 us
  Pallas kernels: 0 us -> 47.6 us
  other arithmetic: 33 us -> 0 us
  blocking collectives: 32.3 us -> 0 us
  waiting for transfers between devices: 18.8 us -> 0 us
  starting transfers between devices: 18.5 us -> 0 us
  matrix products: 15.8 us -> 0 us
    pallas_call x0 -> x1, Pallas kernels: none -> 47.6 us  [on_device(): pl.pallas_call(functools.partial(kernel, (contrib, owners, plane, group,...]
    all_gather x1 -> x0, blocking collectives: 32.3 us -> none  [on_device(): gathered = lax.all_gather(coarse_mesh, 'xy', axis=2, tiled=True)]
    scatter x3 -> x0, local copies, waits for them, and re-layouts: 30.2 us -> none  [the longest x1 14.6 us: on_device(): jnp.zeros((owners * capacity,), jnp.bfloat16).at[slot_of].set(centers)]
    mul x9 -> x0, other arithmetic: 23.4 us -> none  [the longest x8 21.5 us: resample(): picked[:, None, :] * selector[:, :, None]]
    all_to_all x3 -> x0, waiting for transfers between devices: 18.8 us -> none  [the longest x1 14.1 us: on_device(): lax.all_to_all(values.reshape(owners, capacity, voxels), ('xy', 'gz'), sp...]
    all_to_all x3 -> x0, starting transfers between devices: 18.5 us -> none  [the longest x1 6.87 us: on_device(): lax.all_to_all(sent_rows.reshape(owners, capacity), ('xy', 'gz'), split_a...]
    dot_general x6 -> x0, matrix products: 15.8 us -> none  [the longest x1 9.59 us: on_device(): jnp.dot(one_hot, operand, precision=lax.Precision.HIGHEST, preferred_elem...]
    gather x8 -> x0, local copies, waits for them, and re-layouts: 13.5 us -> none  [resample(): picked = jnp.take(source_rows, taps_here[tap_index], axis=0)]
  transfers between devices with their start and end apart: 3 -> 0, of which waited for: 2 -> 0; matrix products, arithmetic and copies ran while one was open for 38% -> 0% of each run, Pallas kernels for 0% -> 0%
where the time goes in v1:
time: 49.4 us; the launch traced here: 49.3 us
  Pallas kernels  47.6 us (96%)
  local copies, waits for them, and re-layouts  1.67 us (3%)
    pallas_call x1, Pallas kernels, on_device(): pl.pallas_call(functools.partial(kernel, (contrib, owners, plane, group,...  47.6 us
    unnamed x1, local copies, waits for them, and re-layouts  1.67 us

profile of v1, /device:TPU:0, one launch (start us, length us, event | category | flops | bytes accessed | tf_op | source)
XLA Modules:
  0.0 49.3 jit_solution(227598749941872744)
XLA Ops:
  0.0 47.6 %shard_map.91 = bf16[1024,128]{1,0:T(8,128)(2,1)} custom-call(bf16[1024,128]{1,0:T(8,128)(2,1)} %source_ref.1, bf16[4096,256]{1,0:T(8,128)(2,1)} %bitcast.4, s32[2,2048]{1,0:T(2,128)} %taps_ref.1, s32[2,2048]{1,0:T(2,128)} %phase_ref.1, s32[1,2048]{1,0:T(1,128)} %bitcast.5, s32[1,2048]{1,0:T(1,128)} %bitcast.6, s32[1,2048]{1,0:T(1,128)} %bitcast.7, ...), custom_call_target="tpu_custom_call" | custom-call | tf_op jit(solution)/shard_map/pallas_call | solution.py:247
  47.6 1.7 %copy.11 = bf16[1024,128]{1,0:T(8,128)(2,1)} copy(bf16[1024,128]{1,0:T(8,128)(2,1)} %shard_map.91) | data formatting | bytes 524288

commit v2 on v1

--- a/solution.py
+++ b/solution.py
@@ -24,6 +24,15 @@
     return out
 
 
+def flip_static(a, b, count):
+    out, bit = a, 1
+    while bit < count:
+        if (b // bit) % 2:
+            out = out + bit - 2 * bit * ((a // bit) % 2)
+        bit *= 2
+    return out
+
+
 def one_hot(columns, values):
     return jnp.where(columns == values, 1.0, 0.0).astype(bf16)
 
@@ -32,12 +41,12 @@
     sizes,
     source_ref, bank_hbm, taps_ref, phase_ref, node_ref, tile_ref, row_ref, owner_ref, mesh_ref,
     out_ref,
-    bank, member, info_rows, info_all, placed, acc, mesh_own, mesh_got, sent, got,
+    spread_src, bank, member, info_rows, info_all, placed, acc, mesh_own, mesh_got, sent, got,
     bank_sem, mesh_send, mesh_recv, send_sem, recv_sem,
 ):
     contrib, owners, plane, group, cap, wide, nodes = sizes
     voxels = source_ref.shape[1]
-    rows_src = source_ref.shape[0]
+    parts_src = source_ref.shape[0] // 256
     tile_rows = out_ref.shape[0]
     phases = placed.shape[1] // (2 * voxels)
     spread = float(voxels // 4)
@@ -50,9 +59,10 @@
 
     barrier = pltpu.get_barrier_semaphore()
 
-    @pl.loop(1, owners)
-    def _(step):
-        pl.semaphore_signal(barrier, inc=1, device_id=device(step), device_id_type=pl.DeviceIdType.MESH)
+    for step in range(1, owners):
+        other = flip_static(me, step, owners)
+        there = (slab_at, other // group, other % group)
+        pl.semaphore_signal(barrier, inc=1, device_id=there, device_id_type=pl.DeviceIdType.MESH)
 
     bank_copy = pltpu.make_async_copy(bank_hbm, bank, bank_sem)
     bank_copy.start()
@@ -62,22 +72,6 @@
         lax.broadcasted_iota(i32, (part, nodes), 1) == lax.broadcasted_iota(i32, (part, nodes), 0) + xy_at * part, 1.0, 0.0
     )
     mesh_own[...] = jnp.dot(mesh_ref[0], place, precision=lax.Precision.HIGHEST, preferred_element_type=f32)
-
-    pl.semaphore_wait(barrier, owners - 1)
-
-    def mesh_copy(step):
-        return pltpu.make_async_remote_copy(
-            src_ref=mesh_own,
-            dst_ref=mesh_got.at[step],
-            send_sem=mesh_send.at[step],
-            recv_sem=mesh_recv.at[step],
-            device_id=(slab_at, flip(xy_at, step, plane), gz_at),
-            device_id_type=pl.DeviceIdType.MESH,
-        )
-
-    @pl.loop(1, plane)
-    def _(step):
-        mesh_copy(step).start()
 
     tiles = tile_ref[...]
     owner = jnp.zeros_like(tiles)
@@ -98,11 +92,25 @@
         ranks.append(jnp.sum(here * earlier, axis=0, keepdims=True))
         carry = carry + jnp.sum(here, axis=1, keepdims=True)
     rank = jnp.concatenate(ranks, axis=1)
+    pl.semaphore_wait(barrier, owners - 1)
+
+    def mesh_copy(step):
+        return pltpu.make_async_remote_copy(
+            src_ref=mesh_own,
+            dst_ref=mesh_got.at[step],
+            send_sem=mesh_send.at[step],
+            recv_sem=mesh_recv.at[step],
+            device_id=(slab_at, flip_static(xy_at, step, plane), gz_at),
+            device_id_type=pl.DeviceIdType.MESH,
+        )
+
+    for step in range(1, plane):
+        mesh_copy(step).start()
+
     rank_hot = one_hot(lax.broadcasted_iota(i32, (wide, contrib), 0).astype(f32), rank)
     node_hot = one_hot(lax.broadcasted_iota(i32, (nodes, contrib), 0), node_ref[...])
 
-    @pl.loop(1, plane)
-    def _(step):
+    for step in range(1, plane):
         mesh_copy(step).wait_recv()
 
     mesh = mesh_own[...]
@@ -134,6 +142,8 @@
             info * member[pl.ds(step, 1), :]
         ).astype(bf16)
 
+    for at in range(parts_src):
+        spread_src[:, at * voxels : (at + 1) * voxels] = source_ref[at * 256 : (at + 1) * 256, :]
     info_all[...] = lax.dot_general(info_rows[...], rank_hot, NT, preferred_element_type=f32)
     acc[...] = jnp.zeros_like(acc)
     bank_copy.wait()
@@ -148,7 +158,7 @@
             device_id_type=pl.DeviceIdType.MESH,
         )
 
-    bundle = max(1, 256 // cap)
+    bundle = max(1, 512 // cap)
     size = bundle * cap
     lines_each = wide // LANES
 
@@ -164,11 +174,15 @@
                 filled = jnp.where(spot == at, line, filled)
             sent[first + d, cap : cap + META, :] = filled.astype(bf16)
         columns = pieces[0] if bundle == 1 else jnp.concatenate(pieces, axis=0)
-        source = source_ref[...]
-        ids = lax.broadcasted_iota(i32, (size, rows_src), 1).astype(f32)
+        ids = lax.broadcasted_iota(i32, (size, 256), 1).astype(f32)
+        hot = jnp.concatenate([one_hot(ids, columns[:, 1:2]), one_hot(ids, columns[:, 3:4])], axis=0)
+        quads = jnp.dot(hot, spread_src[...], preferred_element_type=f32).astype(bf16)
         for k in range(2):
-            tap = columns[:, 2 * k : 2 * k + 1] * 256.0 + columns[:, 2 * k + 1 : 2 * k + 2]
-            picked = jnp.dot(one_hot(ids, tap), source, preferred_element_type=f32).astype(bf16)
+            quad = quads[k * size : (k + 1) * size]
+            high = jnp.broadcast_to(columns[:, 2 * k : 2 * k + 1], (size, voxels)).astype(bf16)
+            picked = quad[:, :voxels]
+            for at in range(1, parts_src):
+                picked = jnp.where(high == jnp.bfloat16(at), quad[:, at * voxels : (at + 1) * voxels], picked)
             phase = jnp.broadcast_to(columns[:, 4 + k : 5 + k], (size, voxels)).astype(bf16)
             for p in range(phases):
                 at = (k * phases + p) * voxels
@@ -184,17 +198,31 @@
             def _():
                 value_copy(first + d).start()
 
-    def consume(values, meta):
-        meta = meta.astype(f32)
-        target = meta[lines_each : 2 * lines_each] * 256.0 + meta[2 * lines_each : 3 * lines_each]
-        target = jnp.concatenate([target[at : at + 1] for at in range(lines_each)], axis=1)[:, :cap]
-        turned = meta.T
-        center = jnp.concatenate([turned[:, at : at + 1] for at in range(lines_each)], axis=0)[:cap]
-        offsets = lax.broadcasted_iota(i32, (cap, voxels), 1).astype(f32) - center
-        weights = jnp.exp(-0.5 * (offsets / spread) ** 2)
-        operand = jnp.concatenate([weights * values.astype(f32), weights], axis=1).astype(bf16)
+            @pl.when(first + d == 0)
+            def _():
+                got[0] = sent[0]
+
+    def consume(first):
+        targets, operands = [], []
+        for d in range(bundle):
+            step = first + d
+
+            @pl.when(step > 0)
+            def _():
+                value_copy(step).wait_recv()
+
+            meta = got[step, cap : cap + META, :].astype(f32)
+            target = meta[lines_each : 2 * lines_each] * 256.0 + meta[2 * lines_each : 3 * lines_each]
+            targets.append(jnp.concatenate([target[at : at + 1] for at in range(lines_each)], axis=1)[:, :cap])
+            turned = meta.T
+            center = jnp.concatenate([turned[:, at : at + 1] for at in range(lines_each)], axis=0)[:cap]
+            offsets = lax.broadcasted_iota(i32, (cap, voxels), 1).astype(f32) - center
+            weights = jnp.exp(-0.5 * (offsets / spread) ** 2)
+            values = got[step, :cap, :].astype(f32)
+            operands.append(jnp.concatenate([weights * values, weights], axis=1).astype(bf16))
         ids = lax.broadcasted_iota(i32, (tile_rows, cap), 0).astype(f32) + 1.0
-        acc[...] += jnp.dot(one_hot(ids, target), operand, preferred_element_type=f32)
+        hot = jnp.concatenate([one_hot(ids, target) for target in targets], axis=1)
+        acc[...] += jnp.dot(hot, jnp.concatenate(operands, axis=0), preferred_element_type=f32)
 
     blocks = owners // bundle
 
@@ -202,18 +230,14 @@
     def _(turn):
         produce((blocks - 1 - turn) * bundle)
 
-    consume(sent[0, :cap, :], sent[0, cap : cap + META, :])
-
-    @pl.loop(1, owners)
+    @pl.loop(0, blocks)
     def _(turn):
-        step = owners - turn
-        value_copy(step).wait_recv()
-        consume(got[step, :cap, :], got[step, cap : cap + META, :])
+        half = blocks // 2
+        consume(jnp.where(turn < half, turn, blocks - 1 - turn + half) * bundle)
 
     out_ref[...] = (acc[:, :voxels] / jnp.maximum(acc[:, voxels:], floor_weight)).astype(bf16)
 
-    @pl.loop(1, plane)
-    def _(step):
+    for step in range(1, plane):
         mesh_copy(step).wait_send()
 
     @pl.loop(1, owners)
@@ -242,7 +266,7 @@
     wide = max(cap, LANES)
     tile_rows = contrib // 2
     nodes = plane * coarse_mesh.shape[2]
-    bundle = max(1, 256 // cap)
+    bundle = max(1, 512 // cap)
     vmem = pl.BlockSpec(memory_space=pltpu.VMEM)
     return pl.pallas_call(
         functools.partial(kernel, (contrib, owners, plane, group, cap, wide, nodes)),
@@ -251,6 +275,7 @@
         + [pl.BlockSpec(memory_space=pltpu.SMEM), vmem],
         out_specs=vmem,
         scratch_shapes=[
+            pltpu.VMEM((256, source_rows.shape[0] // 256 * voxels), bf16),
             pltpu.VMEM((taps * phases * voxels, 2 * voxels), bf16),
             pltpu.VMEM((owners, contrib), f32),
             pltpu.VMEM((owners * INFO, contrib), bf16),

time: 49.4 us -> 42.6 us (0.86)
  Pallas kernels: 47.6 us -> 40.5 us
    pallas_call x1, Pallas kernels: 47.6 us -> 40.5 us  [on_device(): pl.pallas_call(functools.partial(kernel, (contrib, owners, plane, group,...]
where the time goes in v2:
time: 42.6 us; the launch traced here: 42.2 us
  Pallas kernels  40.5 us (95%)
  local copies, waits for them, and re-layouts  1.67 us (4%)
    pallas_call x1, Pallas kernels, on_device(): pl.pallas_call(functools.partial(kernel, (contrib, owners, plane, group,...  40.5 us
    unnamed x1, local copies, waits for them, and re-layouts  1.67 us

profile of v2, /device:TPU:0, one launch (start us, length us, event | category | flops | bytes accessed | tf_op | source)
XLA Modules:
  0.0 42.2 jit_solution(18008160086786301410)
XLA Ops:
  0.0 40.5 %shard_map.91 = bf16[1024,128]{1,0:T(8,128)(2,1)} custom-call(bf16[1024,128]{1,0:T(8,128)(2,1)} %source_ref.1, bf16[4096,256]{1,0:T(8,128)(2,1)} %bitcast.4, s32[2,2048]{1,0:T(2,128)} %taps_ref.1, s32[2,2048]{1,0:T(2,128)} %phase_ref.1, s32[1,2048]{1,0:T(1,128)} %bitcast.5, s32[1,2048]{1,0:T(1,128)} %bitcast.6, s32[1,2048]{1,0:T(1,128)} %bitcast.7, ...), custom_call_target="tpu_custom_call" | custom-call | tf_op jit(solution)/shard_map/pallas_call | solution.py:271
  40.6 1.7 %copy.11 = bf16[1024,128]{1,0:T(8,128)(2,1)} copy(bf16[1024,128]{1,0:T(8,128)(2,1)} %shard_map.91) | data formatting | bytes 524288

commit v3 on v2

--- a/solution.py
+++ b/solution.py
@@ -11,7 +11,6 @@
 LANES = 128
 INFO = 16
 MESH_ROW = 6
-META = 16
 f32, bf16, i32 = jnp.float32, jnp.bfloat16, jnp.int32
 NT = (((1,), (1,)), ((), ()))
 
@@ -41,8 +40,8 @@
     sizes,
     source_ref, bank_hbm, taps_ref, phase_ref, node_ref, tile_ref, row_ref, owner_ref, mesh_ref,
     out_ref,
-    spread_src, bank, member, info_rows, info_all, placed, acc, mesh_own, mesh_got, sent, got,
-    bank_sem, mesh_send, mesh_recv, send_sem, recv_sem,
+    spread_src, bank, member, info_rows, info_all, info_turned, placed, acc, mesh_own, mesh_got, sent, got, notes_sent, notes_got,
+    bank_sem, mesh_send, mesh_recv, send_sem, recv_sem, note_send, note_recv,
 ):
     contrib, owners, plane, group, cap, wide, nodes = sizes
     voxels = source_ref.shape[1]
@@ -145,6 +144,7 @@
     for at in range(parts_src):
         spread_src[:, at * voxels : (at + 1) * voxels] = source_ref[at * 256 : (at + 1) * 256, :]
     info_all[...] = lax.dot_general(info_rows[...], rank_hot, NT, preferred_element_type=f32)
+    info_turned[...] = info_all[...].T
     acc[...] = jnp.zeros_like(acc)
     bank_copy.wait()
 
@@ -158,6 +158,16 @@
             device_id_type=pl.DeviceIdType.MESH,
         )
 
+    def note_copy(step):
+        return pltpu.make_async_remote_copy(
+            src_ref=notes_sent.at[step],
+            dst_ref=notes_got.at[step],
+            send_sem=note_send.at[step],
+            recv_sem=note_recv.at[step],
+            device_id=device(step),
+            device_id_type=pl.DeviceIdType.MESH,
+        )
+
     bundle = max(1, 512 // cap)
     size = bundle * cap
     lines_each = wide // LANES
@@ -166,13 +176,12 @@
         pieces = []
         for d in range(bundle):
             lanes = info_all[pl.ds(pl.multiple_of((first + d) * INFO, INFO), INFO), :]
-            pieces.append(lanes.T[:cap])
-            meta = [lanes[r : r + 1, at * LANES : (at + 1) * LANES] for r in (9, 10, 11) for at in range(lines_each)]
-            spot = lax.broadcasted_iota(i32, (META, LANES), 0)
-            filled = jnp.zeros((META, LANES), f32)
-            for at, line in enumerate(meta):
-                filled = jnp.where(spot == at, line, filled)
-            sent[first + d, cap : cap + META, :] = filled.astype(bf16)
+            width = owners * INFO
+            pieces.append(pltpu.roll(info_turned[:cap, :], (width - (first + d) * INFO) % width, 1))
+            center, target = lanes[9:10], lanes[10:11] * 256.0 + lanes[11:12]
+            for at in range(lines_each):
+                notes_sent[first + d, at : at + 1, :] = center[:, at * LANES : (at + 1) * LANES]
+                notes_sent[first + d, lines_each + at : lines_each + at + 1, :] = target[:, at * LANES : (at + 1) * LANES]
         columns = pieces[0] if bundle == 1 else jnp.concatenate(pieces, axis=0)
         ids = lax.broadcasted_iota(i32, (size, 256), 1).astype(f32)
         hot = jnp.concatenate([one_hot(ids, columns[:, 1:2]), one_hot(ids, columns[:, 3:4])], axis=0)
@@ -196,11 +205,13 @@
 
             @pl.when(first + d > 0)
             def _():
+                note_copy(first + d).start()
                 value_copy(first + d).start()
 
             @pl.when(first + d == 0)
             def _():
                 got[0] = sent[0]
+                notes_got[0] = notes_sent[0]
 
     def consume(first):
         targets, operands = [], []
@@ -209,12 +220,13 @@
 
             @pl.when(step > 0)
             def _():
+                note_copy(step).wait_recv()
                 value_copy(step).wait_recv()
 
-            meta = got[step, cap : cap + META, :].astype(f32)
-            target = meta[lines_each : 2 * lines_each] * 256.0 + meta[2 * lines_each : 3 * lines_each]
+            notes = notes_got[step]
+            target = notes[lines_each:]
             targets.append(jnp.concatenate([target[at : at + 1] for at in range(lines_each)], axis=1)[:, :cap])
-            turned = meta.T
+            turned = notes.T
             center = jnp.concatenate([turned[:, at : at + 1] for at in range(lines_each)], axis=0)[:cap]
             offsets = lax.broadcasted_iota(i32, (cap, voxels), 1).astype(f32) - center
             weights = jnp.exp(-0.5 * (offsets / spread) ** 2)
@@ -228,7 +240,7 @@
 
     @pl.loop(0, blocks)
     def _(turn):
-        produce((blocks - 1 - turn) * bundle)
+        produce((blocks - 1 - turn // 2 - blocks // 2 * (turn % 2)) * bundle)
 
     @pl.loop(0, blocks)
     def _(turn):
@@ -242,6 +254,7 @@
 
     @pl.loop(1, owners)
     def _(step):
+        note_copy(step).wait_send()
         value_copy(step).wait_send()
 
 
@@ -280,15 +293,20 @@
             pltpu.VMEM((owners, contrib), f32),
             pltpu.VMEM((owners * INFO, contrib), bf16),
             pltpu.VMEM((owners * INFO, wide), f32),
+            pltpu.VMEM((wide, owners * INFO), f32),
             pltpu.VMEM((bundle * cap, taps * phases * voxels), bf16),
             pltpu.VMEM((tile_rows, 2 * voxels), f32),
             pltpu.VMEM((2, nodes), f32),
             pltpu.VMEM((plane, 2, nodes), f32),
-            pltpu.VMEM((owners, cap + META, voxels), bf16),
-            pltpu.VMEM((owners, cap + META, voxels), bf16),
+            pltpu.VMEM((owners, cap, voxels), bf16),
+            pltpu.VMEM((owners, cap, voxels), bf16),
+            pltpu.VMEM((owners, 2 * wide // LANES, LANES), f32),
+            pltpu.VMEM((owners, 2 * wide // LANES, LANES), f32),
             pltpu.SemaphoreType.DMA,
             pltpu.SemaphoreType.DMA((plane,)),
             pltpu.SemaphoreType.DMA((plane,)),
+            pltpu.SemaphoreType.DMA((owners,)),
+            pltpu.SemaphoreType.DMA((owners,)),
             pltpu.SemaphoreType.DMA((owners,)),
             pltpu.SemaphoreType.DMA((owners,)),
         ],

time: 42.6 us -> 42.1 us (0.988)
  no operation moved by 1% of the time
where the time goes in v3:
time: 42.1 us; the launch traced here: 42 us
  Pallas kernels  40.3 us (96%)
  local copies, waits for them, and re-layouts  1.67 us (4%)
    pallas_call x1, Pallas kernels, on_device(): pl.pallas_call(functools.partial(kernel, (contrib, owners, plane, group,...  40.3 us
    unnamed x1, local copies, waits for them, and re-layouts  1.67 us

profile of v3, /device:TPU:0, one launch (start us, length us, event | category | flops | bytes accessed | tf_op | source)
XLA Modules:
  0.0 42.0 jit_solution(12356152779247401439)
XLA Ops:
  0.0 40.3 %shard_map.91 = bf16[1024,128]{1,0:T(8,128)(2,1)} custom-call(bf16[1024,128]{1,0:T(8,128)(2,1)} %source_ref.1, bf16[4096,256]{1,0:T(8,128)(2,1)} %bitcast.4, s32[2,2048]{1,0:T(2,128)} %taps_ref.1, s32[2,2048]{1,0:T(2,128)} %phase_ref.1, s32[1,2048]{1,0:T(1,128)} %bitcast.5, s32[1,2048]{1,0:T(1,128)} %bitcast.6, s32[1,2048]{1,0:T(1,128)} %bitcast.7, ...), custom_call_target="tpu_custom_call" | custom-call | tf_op jit(solution)/shard_map/pallas_call | solution.py:284
  40.3 1.7 %copy.11 = bf16[1024,128]{1,0:T(8,128)(2,1)} copy(bf16[1024,128]{1,0:T(8,128)(2,1)} %shard_map.91) | data formatting | bytes 524288
